TPU v7x, 128 devices: a whole 4x4x4 slice. The times are simulated.
128 devices in a mesh: row: 8 (over x, core), col: 16 (over z, y).
Axes of the slice: x: 4, y: 4, z: 4, core: 2. Of those that a mesh axis runs over, the one named last changes fastest.
Arguments:
- markov: bfloat16 [2, 512, 128, 128], P(None, 'col'), may hold values from -6 to 6
- omega: bfloat16 [65536, 64], P('col'), may hold values from -0.0234375 to 0.0234375
Outputs:
- denoised: float32 [2, 512, 128, 128], P(None, 'col')
All inputs are finite; a program needn't handle non-finite values.
Results may differ from a plain program's by a relative error of at most 0.0007.
Values may be sent and summed in bfloat16 or wider, within the bound.
A program may use at most 64 MiB of HBM per device.

v0:
```python
import functools

import jax
import jax.numpy as jnp
from jax import lax
from jax.experimental import pallas as pl
from jax.experimental.pallas import tpu as pltpu
from jax.sharding import PartitionSpec as P

NS_STEPS = 8
norm_floor = 1e-06
highest = lax.Precision.HIGHEST
MESH = pl.DeviceIdType.MESH
KH = 32
B = 128
f32, bf16 = jnp.float32, jnp.bfloat16
NT_DIMS = (((1,), (1,)), ((), ()))


def mm(left, right, **kw):
    return jnp.dot(left, right, preferred_element_type=f32, **kw)


def mm_nt(left, right, **kw):
    return lax.dot_general(left, right, NT_DIMS, preferred_element_type=f32, **kw)


def kernel(
    X, C, nb, SDT,
    l_ref, om_ref, out_ref,
    wl, q, omp, acc, s_send, s_recv, g_own, gx_recv, p_ref,
    bp, bpt, pacc, pr_send, pr_recv, prb, prx, tot, tx_send, tx_recv, ch, xr,
    sg, om, l_sem, om_sem, om_s, om_r, s_s, s_r, sw_s, sw_r, gx_s, gx_r, b_s, b_r,
    pr_s, pr_r, pa_s, pa_r, tx_s, tx_r, xr_s, xr_r, ag_s, ag_r, fx_s, fx_r,
):
    NT = nb // 2
    HB = NT // 2
    PO = nb // C
    PQ = NT // X
    LQ = NT // X
    r = lax.axis_index("row")
    c = lax.axis_index("col")
    x, core = r // 2, r % 2

    def dev(xx, cc, kk=None):
        return (xx * 2 + (core if kk is None else kk), cc)

    def col(dc):
        return lax.rem(c + dc + 4 * C, C)

    def xat(dx):
        return lax.rem(x + dx, X)

    def xcol(dx, delta):
        xx = xat(dx)
        return dev(xx, lax.rem(c + 2 * (xx - x) + delta + 4 * C, C))

    def remote(src, dst, send, recv, device):
        return pltpu.make_async_remote_copy(
            src_ref=src, dst_ref=dst, send_sem=send, recv_sem=recv, device_id=device, device_id_type=MESH
        )

    halves = [jnp.where(c - 2 * x - e < 0, 1, 0).astype(jnp.int32) for e in range(3)]

    barrier = pltpu.get_barrier_semaphore()
    peers = [dev(x, col(dc)) for dc in range(1, C)]
    for dx in range(1, X):
        peers += [xcol(dx, delta) for delta in (-1, 0, 1)] + [dev(xat(dx), c)]
    peers.append(dev(x, c, 1 - core))
    for peer in peers:
        pl.semaphore_signal(barrier, inc=1, device_id=peer, device_id_type=MESH)

    loads = []
    for h in range(2):
        for s in range(2):
            loads.append(
                pltpu.make_async_copy(
                    l_ref.at[h],
                    wl.at[h, pl.ds((1 + s) * B, nb * B), pl.ds(s * B, B)],
                    l_sem.at[2 * h + s],
                )
            )
    for cp in loads:
        cp.start()
    half_rank = pl.ds(pl.multiple_of(core * KH, KH), KH)
    om_load = pltpu.make_async_copy(om_ref.at[half_rank], om, om_sem)
    om_load.start()
    zero = jnp.zeros((B, B), bf16)
    for h in range(2):
        wl[h, 0:B, 0:B] = zero
        wl[h, 0:B, B:] = zero
        wl[h, B : 2 * B, B:] = zero
        wl[h, (nb + 1) * B :, 0:B] = zero
    bp[0 : NT * KH, :] = jnp.zeros((NT * KH, 2 * B), bf16)
    bp[3 * NT * KH :, :] = jnp.zeros((NT * KH, 2 * B), bf16)
    PAD = PQ - 1
    for e in range(3):
        omp[e, 0 : PAD * KH, :] = jnp.zeros((PAD * KH, 2 * B), bf16)
        omp[e, (PAD + NT) * KH :, :] = jnp.zeros((PAD * KH, 2 * B), bf16)
    om_load.wait()
    for w in range(NT):
        n = NT - 1 - w
        q[n * KH : (n + 1) * KH, :B] = om[:, (2 * w + 1) * B : (2 * w + 2) * B]
        q[n * KH : (n + 1) * KH, B:] = om[:, 2 * w * B : (2 * w + 1) * B]
    pl.semaphore_wait(barrier, len(peers))

    pending = []

    om_self = [lax.rem(2 * x + e, C) == 0 for e in range(3)]
    om_copies = []
    for e in range(3):
        cp = remote(q, omp.at[e, pl.ds(PAD * KH, NT * KH)], om_s.at[e], om_r.at[e], dev(x, col(2 * x + e)))
        om_copies.append(cp)

        @pl.when(jnp.logical_not(om_self[e]))
        def _():
            cp.start()

        @pl.when(om_self[e])
        def _():
            omp[e, PAD * KH : (PAD + NT) * KH, :] = q[...]

    for cp in loads:
        cp.wait()

    def lags(e, tau):
        return wl[halves[e], tau * 2 * B : (tau + 1) * 2 * B, :]

    srows, brows = PO * KH, PQ * KH
    s_copies = []

    def send_sketch(first, last):
        for dst in range(first, last):
            dc = lax.rem(dst - c + C, C)
            cp = remote(
                s_send.at[pl.ds(dst * srows, srows)], s_recv.at[dc], s_s.at[dc], s_r.at[dc], dev(x, dst)
            )
            pl.when(dst != c)(cp.start)

    started = set()
    for e in range(3):
        @pl.when(jnp.logical_not(om_self[e]))
        def _():
            om_copies[e].wait_recv()

        for b in range(0, 2 * NT, PQ):
            value = None
            for tau in range(NT + 1):
                n = b + NT - tau - e * NT
                if -PQ < n < NT:
                    left = omp[e, (PAD + n) * KH : (PAD + n) * KH + brows, :]
                    term = mm_nt(left, lags(e, tau))
                    value = term if value is None else value + term
            if value is None:
                continue
            rows = slice(b * KH, b * KH + brows)
            if b in started:
                value = value + acc[rows, :]
            started.add(b)
            acc[rows, :] = value
            if (e == 1 and b < NT) or e == 2:
                s_send[rows, :] = value.astype(SDT)
        if e > 0:
            send_sketch((e - 1) * C // 2, e * C // 2)

    for dc in range(1, C):
        s_copies.append(
            remote(s_send.at[pl.ds(0, srows)], s_recv.at[dc], s_s.at[dc], s_r.at[dc], dev(x, col(dc)))
        )
    total = acc[pl.ds(pl.multiple_of(c * srows, srows), srows), :]
    for dc in range(1, C):
        s_copies[dc - 1].wait_recv()
        total = total + s_recv[dc].astype(f32)
    pending += s_copies
    mine = pl.ds(pl.multiple_of(c * srows, srows), srows)
    sg[core, mine, :] = total.astype(bf16)
    b_copies = {}
    side = 4 if C % 4 == 0 else 1

    def hops(dc):
        y, z = dc % side, dc // side
        return min(y, side - y) + min(z, C // side - z)

    for dc in sorted(range(1, C), key=lambda dc: -hops(dc)):
        b_copies[dc] = remote(sg.at[core, mine], sg.at[core, mine], b_s.at[dc], b_r.at[dc], dev(x, col(dc)))
        b_copies[dc].start()

    def row_pair(n):
        return jnp.concatenate(
            [sg[k, pl.ds(pl.multiple_of(n * KH, KH), KH), :] for k in range(2)], axis=0
        )

    groups = C // side
    group = [lax.rem(c // side + g, groups) for g in range(groups)]
    grows = side * srows
    overs = []
    for g in range(groups):
        for y in range(side):
            dc = lax.rem(c - (group[g] * side + y) + C, C)
            cp = remote(sg.at[core, mine], sg.at[core, mine], b_s.at[dc], b_r.at[dc], dev(x, c, 1 - core))
            pl.when(dc != 0)(cp.wait_recv)
        at = sg.at[core, pl.ds(pl.multiple_of(group[g] * grows, grows), grows)]
        overs.append(remote(at, at, sw_s.at[g], sw_r.at[g], dev(x, c, 1 - core)))
        overs[g].start()
    gram = None
    for g in range(groups):
        overs[g].wait_recv()
        for i in range(side * PO):
            both = row_pair(group[g] * (side * PO) + i)
            term = mm_nt(both, both)
            gram = term if gram is None else gram + term
    g_own[...] = jnp.concatenate([gram[:KH], gram[KH:]], axis=1)
    gx_copies = []
    for dx in range(1, X):
        cp = remote(g_own, gx_recv.at[dx], gx_s.at[dx], gx_r.at[dx], dev(xat(dx), c))
        cp.start()
        gx_copies.append(cp)
    packed = g_own[...]
    for dx in range(1, X):
        gx_copies[dx - 1].wait_recv()
        packed = packed + gx_recv[dx]
    pending += [*b_copies.values(), *overs, *gx_copies]
    gram = jnp.concatenate([packed[:, : 2 * KH], packed[:, 2 * KH :]], axis=0)

    eye = (
        lax.broadcasted_iota(jnp.int32, (2 * KH, 2 * KH), 0)
        == lax.broadcasted_iota(jnp.int32, (2 * KH, 2 * KH), 1)
    ).astype(f32)
    trace = jnp.sum(gram * eye)
    scale = 1.0 / jnp.sqrt(jnp.full((1, 1), trace, f32) + norm_floor)
    inner = gram * (scale * scale)
    prod = None
    for sweep in range(NS_STEPS):
        a = 1.5 * eye - 0.5 * inner
        prod = a if prod is None else mm(prod, a, precision=highest)
        if sweep < NS_STEPS - 1:
            inner = mm(a, mm(inner, a, precision=highest), precision=highest)
    p_ref[...] = prod * scale
    weights = p_ref[half_rank, :]
    w1 = weights.astype(bf16)
    rest = weights - w1.astype(f32)
    w2 = rest.astype(bf16)
    w3 = (rest - w2.astype(f32)).astype(bf16)
    stack = jnp.concatenate([w1, w2, w3], axis=0)
    for n in range(2 * NT):
        three = mm(stack, row_pair(n))
        value = three[:KH] + three[KH : 2 * KH] + three[2 * KH :]
        bp[(NT + n) * KH : (NT + n + 1) * KH, :] = value.astype(bf16)

    qrows = PQ * KH
    pr_copies = {}
    for dx in range(X):
        for e in range(3):
            if dx > 0 or e != 1:
                slot = dx * 3 + e
                pr_copies[slot] = remote(
                    pr_send.at[e, pl.ds(0, qrows)], pr_recv.at[slot], pr_s.at[slot], pr_r.at[slot],
                    xcol(dx, 1 - e),
                )
    for e in (0, 2, 1):
        for b in range(0, NT, PQ):
            value = None
            for tau in range(NT + 1):
                if (e == 0 and b + PQ - 1 < NT - tau) or (e == 2 and b >= NT - tau):
                    continue
                first = (e * NT + b + tau) * KH
                term = mm(bp[first : first + qrows, :], lags(e, tau))
                value = term if value is None else value + term
            rows = slice(b * KH, b * KH + qrows)
            pr_send[e, rows, :] = value.astype(bf16)
            if e == 1:
                pacc[rows, :] = value
            owner = b // PQ
            dx = lax.rem(owner - x + X, X)
            slot = dx * 3 + e
            cp = remote(
                pr_send.at[e, pl.ds(b * KH, qrows)], pr_recv.at[slot], pr_s.at[slot], pr_r.at[slot],
                dev(owner, lax.rem(c + 2 * (owner - x) + 1 - e + 4 * C, C)),
            )
            if e == 1:
                pl.when(owner != x)(cp.start)
            else:
                cp.start()

    for g in range(NT):
        first = (NT + 2 * g) * KH
        pieces = [
            bp[first + o * KH : first + (o + 1) * KH, s * B : (s + 1) * B] for o in range(2) for s in range(2)
        ]
        bpt[:, g * B : (g + 1) * B] = jnp.concatenate(pieces, axis=0).T

    quarter = pl.ds(pl.multiple_of(x * qrows, qrows), qrows)
    total = pacc[quarter, :]
    for slot, cp in pr_copies.items():
        cp.wait_recv()
        total = total + pr_recv[slot].astype(f32)
    pending += list(pr_copies.values())
    prb[1, quarter, :] = total.astype(bf16)
    copies = []
    for dx in sorted(range(X), key=lambda dx: -min(dx, X - dx)):
        for e in range(3):
            if dx == 0 and e == 1:
                continue
            slot = dx * 3 + e
            cp = remote(
                prb.at[1, quarter], prb.at[e, quarter], pa_s.at[slot], pa_r.at[slot], xcol(dx, e - 1)
            )
            cp.start()
            copies.append(cp)
    for cp in copies:
        cp.wait_recv()
    pending += copies

    def active(h, xx):
        return c - 2 * xx >= 0 if h == 0 else c - 2 * xx - 2 < 0

    nbr, nbc = 2 * nb * X, nb * C

    def lag_of(h, t):
        return h * nbc + c * nb + core * NT + t

    def pairs_of(lag, first, last):
        low = jnp.maximum(first, lag - (nbc - 1))
        return jnp.maximum(jnp.minimum(last, lag) - low + 1, 0).astype(f32)

    def measured(h, t):
        return wl[h, pl.ds(pl.multiple_of((core * NT + t + 1) * B, B), B), 0:B].astype(f32)

    order = sorted(range(1, X), key=lambda dx: -min(dx, X - dx)) + [0]
    tx_copies, xr_sends = [], []
    for h in range(2):
        across, sends = [], {}
        for k, dx in enumerate(order):
            across.append(
                remote(
                    tx_send.at[h, k], tx_recv.at[h, k], tx_s.at[h * X + k], tx_r.at[h * X + k],
                    dev(x, c, 1 - core),
                )
            )
            if dx > 0:
                sends[dx] = remote(
                    ch.at[h, k], xr.at[h, dx], xr_s.at[h * X + dx], xr_r.at[h * X + dx], dev(xat(dx), c)
                )
        tx_copies.append(across)
        xr_sends.append(sends)

        @pl.when(active(h, x))
        def _():
            for e in range(3):
                @pl.when(halves[e] == h)
                def _():
                    for i in range(NT):
                        n = e * NT + i
                        pair = prb[e, i * KH : (i + 1) * KH, :]
                        prx[n, 0:KH, :] = pair
                        prx[n, KH:, :B] = pair[:, B:]
                        if n > 0:
                            prx[n - 1, KH:, B:] = pair[:, :B]

                @pl.when(halves[e] != h)
                def _():
                    for i in range(NT):
                        n = e * NT + i
                        prx[n, 0:KH, :] = jnp.zeros((KH, 2 * B), bf16)
                        prx[n, KH:, :B] = jnp.zeros((KH, B), bf16)
                        if n > 0:
                            prx[n - 1, KH:, B:] = jnp.zeros((KH, B), bf16)

            def lag_pair(tp):
                right = prx[pl.ds(NT - 1 - tp, 2 * NT)].reshape(4 * NT * KH, 2 * B)
                return mm(bpt[...], right)

            def combine(k):
                dx = order[k]
                across[k].wait_recv()
                for i in range(LQ):
                    t = xat(dx) * LQ + i
                    n = pairs_of(lag_of(h, t), 2 * nb * x, 2 * nb * (x + 1) - 1)
                    value = tot[h, k, i] + tx_recv[h, k, i].astype(f32) - (0.5 * n) * measured(h, t)
                    if dx > 0:
                        ch[h, k, i] = value.astype(bf16)
                    else:
                        tot[h, k, i] = value
                if dx > 0:
                    sends[dx].start()

            for k, dx in enumerate(order):
                first = xat(dx) * (LQ // 2)
                for i in range(LQ // 2):
                    value = lag_pair((1 - core) * HB + first + i).astype(bf16)
                    tx_send[h, k, 2 * i] = value[:, B:]
                    tx_send[h, k, 2 * i + 1] = value[:, :B]
                across[k].start()
                for i in range(LQ // 2):
                    value = lag_pair(core * HB + first + i)
                    tot[h, k, 2 * i] = value[:, B:]
                    tot[h, k, 2 * i + 1] = value[:, :B]
                if k > 0:
                    combine(k - 1)
            combine(X - 1)

    has = [None, c < 2 * X]
    ag_copies, fx_copies = [], []

    def piece(h, xx):
        return out_ref.at[h, pl.ds(core * NT + xx * LQ, LQ)]

    for h in range(2):
        ag_copies.append(
            [
                remote(piece(h, x), piece(h, x), ag_s.at[h * X + dx], ag_r.at[h * X + dx], dev(xat(dx), c))
                for dx in range(1, X)
            ]
        )
        fx_copies.append(
            [
                remote(
                    piece(h, lax.rem(x - dx + X, X)), piece(h, lax.rem(x - dx + X, X)),
                    fx_s.at[h * X + dx], fx_r.at[h * X + dx], dev(x, c, 1 - core),
                )
                for dx in range(X)
            ]
        )

    def spread(h):
        @pl.when(jnp.logical_not(active(h, x)))
        def _():
            tot[h, X - 1] = jnp.zeros((LQ, B, B), f32)

        for dx in range(1, X):
            @pl.when(active(h, lax.rem(x - dx + X, X)))
            def _():
                xr_sends[h][dx].wait_recv()
                tot[h, X - 1] += xr[h, dx].astype(f32)

        for i in range(LQ):
            t = x * LQ + i
            n = pairs_of(lag_of(h, t), 0, nbr - 1)
            value = tot[h, X - 1, i] * (1.0 / jnp.maximum(n, 1.0))
            value = value + jnp.where(n > 0, 0.0, 0.5) * measured(h, t)
            out_ref[h, core * NT + t] = value.astype(bf16)
        for cp in ag_copies[h]:
            cp.start()
        fx_copies[h][0].start()

    def gather(h):
        for dx in range(1, X):
            ag_copies[h][dx - 1].wait_recv()
            fx_copies[h][dx].start()

    def settle(h):
        for cp in fx_copies[h]:
            cp.wait_recv()
        for cp in ag_copies[h] + fx_copies[h]:
            cp.wait_send()

    for part in (spread, gather, settle):
        part(0)
        pl.when(has[1])(functools.partial(part, 1))

    @pl.when(jnp.logical_not(has[1]))
    def _():
        for t in range(nb):
            out_ref[1, t] = (0.5 * wl[1, (t + 1) * B : (t + 2) * B, 0:B].astype(f32)).astype(bf16)

    for h in range(2):
        @pl.when(active(h, x))
        def _():
            for cp in tx_copies[h] + list(xr_sends[h].values()):
                cp.wait_send()

    for e in range(3):
        @pl.when(jnp.logical_not(om_self[e]))
        def _():
            om_copies[e].wait_send()

    for cp in pending:
        cp.wait_send()


def local(X, C, SDT, markov, omega):
    halves, nb = markov.shape[:2]
    NT = nb // 2
    PO, PQ, LQ = nb // C, NT // X, NT // X
    vmem, dma = pltpu.VMEM, pltpu.SemaphoreType.DMA
    scratch = [
        vmem((2, (nb + 2) * B, 2 * B), bf16),
        vmem((NT * KH, 2 * B), bf16),
        vmem((3, (NT + 2 * PQ - 2) * KH, 2 * B), bf16),
        vmem((2 * NT * KH, 2 * B), f32),
        vmem((2 * NT * KH, 2 * B), SDT),
        vmem((C, PO * KH, 2 * B), SDT),
        vmem((KH, 4 * KH), f32),
        vmem((X, KH, 4 * KH), f32),
        vmem((2 * KH, 2 * KH), f32),
        vmem((4 * NT * KH, 2 * B), bf16),
        vmem((B, NT * B), bf16),
        vmem((NT * KH, 2 * B), f32),
        vmem((3, NT * KH, 2 * B), bf16),
        vmem((3 * X, PQ * KH, 2 * B), bf16),
        vmem((3, NT * KH, 2 * B), bf16),
        vmem((3 * NT, 2 * KH, 2 * B), bf16),
        vmem((2, X, LQ, B, B), f32),
        vmem((2, X, LQ, B, B), bf16),
        vmem((2, X, LQ, B, B), bf16),
        vmem((2, X, LQ, B, B), bf16),
        vmem((2, X, LQ, B, B), bf16),
        vmem((2, 2 * NT * KH, 2 * B), bf16),
        vmem((KH, nb * B), bf16),
        dma((4,)), dma,
        dma((3,)), dma((3,)), dma((C,)), dma((C,)), dma((C,)), dma((C,)),
        dma((X,)), dma((X,)), dma((C,)), dma((C,)),
        dma((3 * X,)), dma((3 * X,)), dma((3 * X,)), dma((3 * X,)),
        *[dma((2 * X,))] * 8,
    ]
    excess = pl.pallas_call(
        functools.partial(kernel, X, C, nb, SDT),
        out_shape=pltpu.VMEM((halves, nb, B, B), bf16),
        in_specs=[pl.BlockSpec(memory_space=pltpu.HBM)] * 2,
        out_specs=pl.BlockSpec(memory_space=pltpu.VMEM),
        scratch_shapes=scratch,
        compiler_params=pltpu.CompilerParams(
            collective_id=0, has_side_effects=True, vmem_limit_bytes=57 * 2**20
        ),
        name="cadzow",
    )(markov.reshape(halves, nb * B, B), omega.T)
    return 0.75 * markov.astype(f32) + 0.5 * excess.astype(f32)


def solution(mesh):
    X, C = mesh.shape["row"] // 2, mesh.shape["col"]
    in_specs = (P(None, "col", None, None), P("col", None))
    return jax.shard_map(
        functools.partial(local, X, C, bf16),
        mesh=mesh,
        in_specs=in_specs,
        out_specs=P(None, "col", None, None),
        check_vma=False,
    )
```

profile of v0, /device:TPU:33, one launch (start us, length us, event | category | flops | bytes accessed | tf_op | source)
XLA Modules:
  0.0 116.4 jit_solution(2018010638040937196)
XLA Ops:
  0.0 0.0 copy-start
  0.0 113.5 %cadzow.1 = bf16[2,32,128,128]{3,2,1,0:T(8,128)(2,1)S(1)} custom-call(bf16[2,4096,128]{2,1,0:T(8,128)(2,1)} %bitcast.2, bf16[64,4096]{1,0:T(8,128)(2,1)} %bitcast.3), custom_call_target="tpu_custom_call" | custom-call | tf_op jit(solution)/shard_map/cadzow/pallas_call | solution.py:516
  113.5 0.0 copy-done
  113.6 2.9 %multiply_add_fusion = f32[2,32,128,128]{3,2,1,0:T(8,128)} fusion(bf16[2,32,128,128]{3,2,1,0:T(8,128)(2,1)S(1)} %cadzow.1, bf16[2,32,128,128]{3,2,1,0:T(8,128)(2,1)S(1)} %copy-done), kind=kLoop, calls=%fused_computation | loop fusion | flops 5242880 | bytes 8388608 | tf_op jit(solution)/shard_map/add | solution.py:527
Async XLA Ops:
  0.0 113.5 %copy-start = (bf16[2,32,128,128]{3,2,1,0:T(8,128)(2,1)S(1)}, bf16[2,32,128,128]{3,2,1,0:T(8,128)(2,1)}, u32[]{:S(2)}) copy-start(bf16[2,32,128,128]{3,2,1,0:T(8,128)(2,1)} %param.2) | copy-start | bytes 6291460
where the time goes:
time: 119 us; the launch traced here: 116 us
  Pallas kernels  114 us (96%)
  other arithmetic  2.87 us (2%)
    pallas_call x1, Pallas kernels, local(): pl.pallas_call(functools.partial(kernel, X, C, nb, SDT), out_shape=pltpu....  114 us
    add x1, other arithmetic, local(): return 0.75 * markov.astype(f32) + 0.5 * excess.astype(f32)  2.87 us

commit v1 on v0

--- a/solution.py
+++ b/solution.py
@@ -63,10 +63,17 @@
     halves = [jnp.where(c - 2 * x - e < 0, 1, 0).astype(jnp.int32) for e in range(3)]
 
     barrier = pltpu.get_barrier_semaphore()
-    peers = [dev(x, col(dc)) for dc in range(1, C)]
-    for dx in range(1, X):
-        peers += [xcol(dx, delta) for delta in (-1, 0, 1)] + [dev(xat(dx), c)]
-    peers.append(dev(x, c, 1 - core))
+    side = 4 if C % 4 == 0 else 1
+
+    def hops(dc):
+        y, z = dc % side, dc // side
+        return min(y, side - y) + min(z, C // side - z)
+
+    far_cols = sorted(range(1, C), key=lambda dc: -hops(dc))
+    far_x = sorted(range(1, X), key=lambda dx: -min(dx, X - dx))
+    peers = [xcol(dx, delta) for dx in far_x for delta in (-1, 0, 1)]
+    peers += [dev(x, col(dc)) for dc in far_cols]
+    peers += [dev(xat(dx), c) for dx in far_x] + [dev(x, c, 1 - core)]
     for peer in peers:
         pl.semaphore_signal(barrier, inc=1, device_id=peer, device_id_type=MESH)
 
@@ -175,13 +182,7 @@
     mine = pl.ds(pl.multiple_of(c * srows, srows), srows)
     sg[core, mine, :] = total.astype(bf16)
     b_copies = {}
-    side = 4 if C % 4 == 0 else 1
-
-    def hops(dc):
-        y, z = dc % side, dc // side
-        return min(y, side - y) + min(z, C // side - z)
-
-    for dc in sorted(range(1, C), key=lambda dc: -hops(dc)):
+    for dc in far_cols:
         b_copies[dc] = remote(sg.at[core, mine], sg.at[core, mine], b_s.at[dc], b_r.at[dc], dev(x, col(dc)))
         b_copies[dc].start()
 
@@ -366,9 +367,10 @@
                         if n > 0:
                             prx[n - 1, KH:, B:] = jnp.zeros((KH, B), bf16)
 
-            def lag_pair(tp):
-                right = prx[pl.ds(NT - 1 - tp, 2 * NT)].reshape(4 * NT * KH, 2 * B)
-                return mm(bpt[...], right)
+            def lag_pair(tp, first, count):
+                depth = 2 * NT * KH
+                right = prx[pl.ds(NT - 1 - tp + first * NT, count * NT)].reshape(count * depth, 2 * B)
+                return mm(bpt[:, first * depth : (first + count) * depth], right)
 
             def combine(k):
                 dx = order[k]
@@ -384,20 +386,24 @@
                 if dx > 0:
                     sends[dx].start()
 
-            for k, dx in enumerate(order):
-                first = xat(dx) * (LQ // 2)
-                for i in range(LQ // 2):
-                    value = lag_pair((1 - core) * HB + first + i).astype(bf16)
-                    tx_send[h, k, 2 * i] = value[:, B:]
-                    tx_send[h, k, 2 * i + 1] = value[:, :B]
-                across[k].start()
-                for i in range(LQ // 2):
-                    value = lag_pair(core * HB + first + i)
-                    tot[h, k, 2 * i] = value[:, B:]
-                    tot[h, k, 2 * i + 1] = value[:, :B]
-                if k > 0:
-                    combine(k - 1)
-            combine(X - 1)
+            def pipeline(*rows):
+                for k, dx in enumerate(order):
+                    first = xat(dx) * (LQ // 2)
+                    for i in range(LQ // 2):
+                        value = lag_pair((1 - core) * HB + first + i, *rows).astype(bf16)
+                        tx_send[h, k, 2 * i] = value[:, B:]
+                        tx_send[h, k, 2 * i + 1] = value[:, :B]
+                    across[k].start()
+                    for i in range(LQ // 2):
+                        value = lag_pair(core * HB + first + i, *rows)
+                        tot[h, k, 2 * i] = value[:, B:]
+                        tot[h, k, 2 * i + 1] = value[:, :B]
+                    if k > 0:
+                        combine(k - 1)
+                combine(X - 1)
+
+            pl.when(halves[1] == h)(functools.partial(pipeline, 0, 2))
+            pl.when(halves[1] != h)(functools.partial(pipeline, h, 1))
 
     has = [None, c < 2 * X]
     ag_copies, fx_copies = [], []

time: 119 us -> 120 us (level)
  the two profiles are of different devices: /device:TPU:33 before, /device:TPU:5 now
where the time goes in v1:
time: 120 us
  Pallas kernels  117 us (98%)
  other arithmetic  2.87 us (2%)
    pallas_call x1, Pallas kernels, local(): pl.pallas_call(functools.partial(kernel, X, C, nb, SDT), out_shape=pltpu....  117 us
    add x1, other arithmetic, local(): return 0.75 * markov.astype(f32) + 0.5 * excess.astype(f32)  2.87 us

profile of v1, /device:TPU:5, one launch (start us, length us, event | category | flops | bytes accessed | tf_op | source)
XLA Modules:
  0.0 119.5 jit_solution(17810273783919445338)
XLA Ops:
  0.0 0.0 copy-start
  0.0 116.6 %cadzow.1 = bf16[2,32,128,128]{3,2,1,0:T(8,128)(2,1)S(1)} custom-call(bf16[2,4096,128]{2,1,0:T(8,128)(2,1)} %bitcast.2, bf16[64,4096]{1,0:T(8,128)(2,1)} %bitcast.3), custom_call_target="tpu_custom_call" | custom-call | tf_op jit(solution)/shard_map/cadzow/pallas_call | solution.py:522
  116.6 0.0 copy-done
  116.7 2.9 %multiply_add_fusion = f32[2,32,128,128]{3,2,1,0:T(8,128)} fusion(bf16[2,32,128,128]{3,2,1,0:T(8,128)(2,1)S(1)} %cadzow.1, bf16[2,32,128,128]{3,2,1,0:T(8,128)(2,1)S(1)} %copy-done), kind=kLoop, calls=%fused_computation | loop fusion | flops 5242880 | bytes 8388608 | tf_op jit(solution)/shard_map/add | solution.py:533
Async XLA Ops:
  0.0 116.7 %copy-start = (bf16[2,32,128,128]{3,2,1,0:T(8,128)(2,1)S(1)}, bf16[2,32,128,128]{3,2,1,0:T(8,128)(2,1)}, u32[]{:S(2)}) copy-start(bf16[2,32,128,128]{3,2,1,0:T(8,128)(2,1)} %param.2) | copy-start | bytes 6291460

commit v2 on v0

--- a/solution.py
+++ b/solution.py
@@ -30,7 +30,7 @@
     l_ref, om_ref, out_ref,
     wl, q, omp, acc, s_send, s_recv, g_own, gx_recv, p_ref,
     bp, bpt, pacc, pr_send, pr_recv, prb, prx, tot, tx_send, tx_recv, ch, xr,
-    sg, om, l_sem, om_sem, om_s, om_r, s_s, s_r, sw_s, sw_r, gx_s, gx_r, b_s, b_r,
+    sg, om, sp, rfull, rf_s, rf_r, l_sem, om_sem, om_s, om_r, s_s, s_r, sw_s, sw_r, gx_s, gx_r, b_s, b_r,
     pr_s, pr_r, pa_s, pa_r, tx_s, tx_r, xr_s, xr_r, ag_s, ag_r, fx_s, fx_r,
 ):
     NT = nb // 2
@@ -91,8 +91,8 @@
         wl[h, 0:B, B:] = zero
         wl[h, B : 2 * B, B:] = zero
         wl[h, (nb + 1) * B :, 0:B] = zero
-    bp[0 : NT * KH, :] = jnp.zeros((NT * KH, 2 * B), bf16)
-    bp[3 * NT * KH :, :] = jnp.zeros((NT * KH, 2 * B), bf16)
+    sp[0 : NT * KH, :] = jnp.zeros((NT * KH, 2 * B), bf16)
+    sp[3 * NT * KH :, :] = jnp.zeros((NT * KH, 2 * B), bf16)
     PAD = PQ - 1
     for e in range(3):
         omp[e, 0 : PAD * KH, :] = jnp.zeros((PAD * KH, 2 * B), bf16)
@@ -215,11 +215,29 @@
         cp = remote(g_own, gx_recv.at[dx], gx_s.at[dx], gx_r.at[dx], dev(xat(dx), c))
         cp.start()
         gx_copies.append(cp)
+    sp[NT * KH : 3 * NT * KH, :] = sg[core]
+    qrows = PQ * KH
+    swaps = []
+    for e in (0, 2, 1):
+        for b in range(0, NT, PQ):
+            value = None
+            for tau in range(NT + 1):
+                if (e == 0 and b + PQ - 1 < NT - tau) or (e == 2 and b >= NT - tau):
+                    continue
+                first = (e * NT + b + tau) * KH
+                term = mm(sp[first : first + qrows, :], lags(e, tau))
+                value = term if value is None else value + term
+            rfull[core, e, b * KH : b * KH + qrows, :] = value
+        at = rfull.at[core, e]
+        cp = remote(at, at, rf_s.at[e], rf_r.at[e], dev(x, c, 1 - core))
+        cp.start()
+        swaps.append(cp)
+
     packed = g_own[...]
     for dx in range(1, X):
         gx_copies[dx - 1].wait_recv()
         packed = packed + gx_recv[dx]
-    pending += [*b_copies.values(), *overs, *gx_copies]
+    pending += [*b_copies.values(), *overs, *gx_copies, *swaps]
     gram = jnp.concatenate([packed[:, : 2 * KH], packed[:, 2 * KH :]], axis=0)
 
     eye = (
@@ -242,12 +260,7 @@
     w2 = rest.astype(bf16)
     w3 = (rest - w2.astype(f32)).astype(bf16)
     stack = jnp.concatenate([w1, w2, w3], axis=0)
-    for n in range(2 * NT):
-        three = mm(stack, row_pair(n))
-        value = three[:KH] + three[KH : 2 * KH] + three[2 * KH :]
-        bp[(NT + n) * KH : (NT + n + 1) * KH, :] = value.astype(bf16)
-
-    qrows = PQ * KH
+
     pr_copies = {}
     for dx in range(X):
         for e in range(3):
@@ -257,16 +270,18 @@
                     pr_send.at[e, pl.ds(0, qrows)], pr_recv.at[slot], pr_s.at[slot], pr_r.at[slot],
                     xcol(dx, 1 - e),
                 )
-    for e in (0, 2, 1):
+    for k, e in enumerate((0, 2, 1)):
+        swaps[k].wait_recv()
         for b in range(0, NT, PQ):
-            value = None
-            for tau in range(NT + 1):
-                if (e == 0 and b + PQ - 1 < NT - tau) or (e == 2 and b >= NT - tau):
-                    continue
-                first = (e * NT + b + tau) * KH
-                term = mm(bp[first : first + qrows, :], lags(e, tau))
-                value = term if value is None else value + term
             rows = slice(b * KH, b * KH + qrows)
+            pieces = []
+            for n in range(b, b + PQ):
+                both = jnp.concatenate([rfull[m, e, n * KH : (n + 1) * KH, :] for m in range(2)], axis=0)
+                high = both.astype(bf16)
+                low = (both - high.astype(f32)).astype(bf16)
+                three = mm(stack, high)
+                pieces.append(three[:KH] + three[KH : 2 * KH] + (three[2 * KH :] + mm(w1, low)))
+            value = jnp.concatenate(pieces, axis=0)
             pr_send[e, rows, :] = value.astype(bf16)
             if e == 1:
                 pacc[rows, :] = value
@@ -282,6 +297,10 @@
             else:
                 cp.start()
 
+    for n in range(2 * NT):
+        three = mm(stack, row_pair(n))
+        value = three[:KH] + three[KH : 2 * KH] + three[2 * KH :]
+        bp[(NT + n) * KH : (NT + n + 1) * KH, :] = value.astype(bf16)
     for g in range(NT):
         first = (NT + 2 * g) * KH
         pieces = [
@@ -507,6 +526,9 @@
         vmem((2, X, LQ, B, B), bf16),
         vmem((2, 2 * NT * KH, 2 * B), bf16),
         vmem((KH, nb * B), bf16),
+        vmem((4 * NT * KH, 2 * B), bf16),
+        vmem((2, 3, NT * KH, 2 * B), f32),
+        dma((3,)), dma((3,)),
         dma((4,)), dma,
         dma((3,)), dma((3,)), dma((C,)), dma((C,)), dma((C,)), dma((C,)),
         dma((X,)), dma((X,)), dma((C,)), dma((C,)),

time: 119 us -> 118 us (level); the launches traced: 116 us -> 117 us
  no operation moved by 1% of the time
where the time goes in v2:
time: 118 us; the launch traced here: 117 us
  Pallas kernels  114 us (97%)
  other arithmetic  2.87 us (2%)
    pallas_call x1, Pallas kernels, local(): pl.pallas_call(functools.partial(kernel, X, C, nb, SDT), out_shape=pltpu....  114 us
    add x1, other arithmetic, local(): return 0.75 * markov.astype(f32) + 0.5 * excess.astype(f32)  2.87 us

profile of v2, /device:TPU:33, one launch (start us, length us, event | category | flops | bytes accessed | tf_op | source)
XLA Modules:
  0.0 117.0 jit_solution(1835421740039593324)
XLA Ops:
  0.0 0.0 copy-start
  0.0 114.2 %cadzow.1 = bf16[2,32,128,128]{3,2,1,0:T(8,128)(2,1)S(1)} custom-call(bf16[2,4096,128]{2,1,0:T(8,128)(2,1)} %bitcast.2, bf16[64,4096]{1,0:T(8,128)(2,1)} %bitcast.3), custom_call_target="tpu_custom_call" | custom-call | tf_op jit(solution)/shard_map/cadzow/pallas_call | solution.py:538
  114.2 0.0 copy-done
  114.2 2.9 %multiply_add_fusion = f32[2,32,128,128]{3,2,1,0:T(8,128)} fusion(bf16[2,32,128,128]{3,2,1,0:T(8,128)(2,1)S(1)} %cadzow.1, bf16[2,32,128,128]{3,2,1,0:T(8,128)(2,1)S(1)} %copy-done), kind=kLoop, calls=%fused_computation | loop fusion | flops 5242880 | bytes 8388608 | tf_op jit(solution)/shard_map/add | solution.py:549
Async XLA Ops:
  0.0 114.2 %copy-start = (bf16[2,32,128,128]{3,2,1,0:T(8,128)(2,1)S(1)}, bf16[2,32,128,128]{3,2,1,0:T(8,128)(2,1)}, u32[]{:S(2)}) copy-start(bf16[2,32,128,128]{3,2,1,0:T(8,128)(2,1)} %param.2) | copy-start | bytes 6291460

commit v3 on v2

--- a/solution.py
+++ b/solution.py
@@ -130,10 +130,11 @@
     s_copies = []
 
     def send_sketch(first, last):
-        for dst in range(first, last):
+        for i in range(last - first):
+            dst = first + lax.rem(c + i, last - first)
             dc = lax.rem(dst - c + C, C)
             cp = remote(
-                s_send.at[pl.ds(dst * srows, srows)], s_recv.at[dc], s_s.at[dc], s_r.at[dc], dev(x, dst)
+                s_send.at[pl.ds(pl.multiple_of(dst * srows, srows), srows)], s_recv.at[dc], s_s.at[dc], s_r.at[dc], dev(x, dst)
             )
             pl.when(dst != c)(cp.start)
 
@@ -262,40 +263,31 @@
     stack = jnp.concatenate([w1, w2, w3], axis=0)
 
     pr_copies = {}
-    for dx in range(X):
-        for e in range(3):
-            if dx > 0 or e != 1:
-                slot = dx * 3 + e
-                pr_copies[slot] = remote(
-                    pr_send.at[e, pl.ds(0, qrows)], pr_recv.at[slot], pr_s.at[slot], pr_r.at[slot],
-                    xcol(dx, 1 - e),
-                )
+    quarter = pl.ds(pl.multiple_of(x * qrows, qrows), qrows)
     for k, e in enumerate((0, 2, 1)):
         swaps[k].wait_recv()
-        for b in range(0, NT, PQ):
-            rows = slice(b * KH, b * KH + qrows)
+        for dx in sorted(range(X), key=lambda dx: -min(dx, X - dx)):
+            first = xat(dx) * qrows
+            rows = pl.ds(pl.multiple_of(first, qrows), qrows)
             pieces = []
-            for n in range(b, b + PQ):
-                both = jnp.concatenate([rfull[m, e, n * KH : (n + 1) * KH, :] for m in range(2)], axis=0)
+            for n in range(PQ):
+                at = pl.ds(pl.multiple_of(first + n * KH, KH), KH)
+                both = jnp.concatenate([rfull[m, e, at, :] for m in range(2)], axis=0)
                 high = both.astype(bf16)
                 low = (both - high.astype(f32)).astype(bf16)
                 three = mm(stack, high)
                 pieces.append(three[:KH] + three[KH : 2 * KH] + (three[2 * KH :] + mm(w1, low)))
             value = jnp.concatenate(pieces, axis=0)
+            if dx == 0 and e == 1:
+                pacc[...] = value
+                continue
             pr_send[e, rows, :] = value.astype(bf16)
-            if e == 1:
-                pacc[rows, :] = value
-            owner = b // PQ
-            dx = lax.rem(owner - x + X, X)
             slot = dx * 3 + e
             cp = remote(
-                pr_send.at[e, pl.ds(b * KH, qrows)], pr_recv.at[slot], pr_s.at[slot], pr_r.at[slot],
-                dev(owner, lax.rem(c + 2 * (owner - x) + 1 - e + 4 * C, C)),
+                pr_send.at[e, rows], pr_recv.at[slot], pr_s.at[slot], pr_r.at[slot], xcol(dx, 1 - e)
             )
-            if e == 1:
-                pl.when(owner != x)(cp.start)
-            else:
-                cp.start()
+            cp.start()
+            pr_copies[slot] = cp
 
     for n in range(2 * NT):
         three = mm(stack, row_pair(n))
@@ -308,8 +300,7 @@
         ]
         bpt[:, g * B : (g + 1) * B] = jnp.concatenate(pieces, axis=0).T
 
-    quarter = pl.ds(pl.multiple_of(x * qrows, qrows), qrows)
-    total = pacc[quarter, :]
+    total = pacc[...]
     for slot, cp in pr_copies.items():
         cp.wait_recv()
         total = total + pr_recv[slot].astype(f32)
@@ -514,7 +505,7 @@
         vmem((2 * KH, 2 * KH), f32),
         vmem((4 * NT * KH, 2 * B), bf16),
         vmem((B, NT * B), bf16),
-        vmem((NT * KH, 2 * B), f32),
+        vmem((PQ * KH, 2 * B), f32),
         vmem((3, NT * KH, 2 * B), bf16),
         vmem((3 * X, PQ * KH, 2 * B), bf16),
         vmem((3, NT * KH, 2 * B), bf16),

time: 118 us -> 120 us (1.017)
  Pallas kernels: 114 us -> 116 us
    pallas_call x1, Pallas kernels: 114 us -> 116 us  [local(): pl.pallas_call(functools.partial(kernel, X, C, nb, SDT), out_shape=pltpu....]
where the time goes in v3:
time: 120 us; the launch traced here: 119 us
  Pallas kernels  116 us (97%)
  other arithmetic  2.87 us (2%)
    pallas_call x1, Pallas kernels, local(): pl.pallas_call(functools.partial(kernel, X, C, nb, SDT), out_shape=pltpu....  116 us
    add x1, other arithmetic, local(): return 0.75 * markov.astype(f32) + 0.5 * excess.astype(f32)  2.87 us

profile of v3, /device:TPU:33, one launch (start us, length us, event | category | flops | bytes accessed | tf_op | source)
XLA Modules:
  0.0 118.5 jit_solution(1377568161419425187)
XLA Ops:
  0.0 0.0 copy-start
  0.0 115.7 %cadzow.1 = bf16[2,32,128,128]{3,2,1,0:T(8,128)(2,1)S(1)} custom-call(bf16[2,4096,128]{2,1,0:T(8,128)(2,1)} %bitcast.2, bf16[64,4096]{1,0:T(8,128)(2,1)} %bitcast.3), custom_call_target="tpu_custom_call" | custom-call | tf_op jit(solution)/shard_map/cadzow/pallas_call | solution.py:529
  115.7 0.0 copy-done
  115.7 2.9 %multiply_add_fusion = f32[2,32,128,128]{3,2,1,0:T(8,128)} fusion(bf16[2,32,128,128]{3,2,1,0:T(8,128)(2,1)S(1)} %cadzow.1, bf16[2,32,128,128]{3,2,1,0:T(8,128)(2,1)S(1)} %copy-done), kind=kLoop, calls=%fused_computation | loop fusion | flops 5242880 | bytes 8388608 | tf_op jit(solution)/shard_map/add | solution.py:540
Async XLA Ops:
  0.0 115.7 %copy-start = (bf16[2,32,128,128]{3,2,1,0:T(8,128)(2,1)S(1)}, bf16[2,32,128,128]{3,2,1,0:T(8,128)(2,1)}, u32[]{:S(2)}) copy-start(bf16[2,32,128,128]{3,2,1,0:T(8,128)(2,1)} %param.2) | copy-start | bytes 6291460

commit v4 on v2

--- a/solution.py
+++ b/solution.py
@@ -63,10 +63,17 @@
     halves = [jnp.where(c - 2 * x - e < 0, 1, 0).astype(jnp.int32) for e in range(3)]
 
     barrier = pltpu.get_barrier_semaphore()
-    peers = [dev(x, col(dc)) for dc in range(1, C)]
-    for dx in range(1, X):
-        peers += [xcol(dx, delta) for delta in (-1, 0, 1)] + [dev(xat(dx), c)]
-    peers.append(dev(x, c, 1 - core))
+    side = 4 if C % 4 == 0 else 1
+
+    def hops(dc):
+        y, z = dc % side, dc // side
+        return min(y, side - y) + min(z, C // side - z)
+
+    far_cols = sorted(range(1, C), key=lambda dc: -hops(dc))
+    far_x = sorted(range(1, X), key=lambda dx: -min(dx, X - dx))
+    peers = [xcol(dx, delta) for dx in far_x for delta in (-1, 0, 1)]
+    peers += [dev(x, col(dc)) for dc in far_cols]
+    peers += [dev(xat(dx), c) for dx in far_x] + [dev(x, c, 1 - core)]
     for peer in peers:
         pl.semaphore_signal(barrier, inc=1, device_id=peer, device_id_type=MESH)
 
@@ -175,13 +182,7 @@
     mine = pl.ds(pl.multiple_of(c * srows, srows), srows)
     sg[core, mine, :] = total.astype(bf16)
     b_copies = {}
-    side = 4 if C % 4 == 0 else 1
-
-    def hops(dc):
-        y, z = dc % side, dc // side
-        return min(y, side - y) + min(z, C // side - z)
-
-    for dc in sorted(range(1, C), key=lambda dc: -hops(dc)):
+    for dc in far_cols:
         b_copies[dc] = remote(sg.at[core, mine], sg.at[core, mine], b_s.at[dc], b_r.at[dc], dev(x, col(dc)))
         b_copies[dc].start()
 

time: 118 us -> 126 us (1.068)
  Pallas kernels: 114 us -> 122 us
    pallas_call x1, Pallas kernels: 114 us -> 122 us  [local(): pl.pallas_call(functools.partial(kernel, X, C, nb, SDT), out_shape=pltpu....]
where the time goes in v4:
time: 126 us; the launch traced here: 125 us
  Pallas kernels  122 us (97%)
  other arithmetic  2.87 us (2%)
    pallas_call x1, Pallas kernels, local(): pl.pallas_call(functools.partial(kernel, X, C, nb, SDT), out_shape=pltpu....  122 us
    add x1, other arithmetic, local(): return 0.75 * markov.astype(f32) + 0.5 * excess.astype(f32)  2.87 us

profile of v4, /device:TPU:33, one launch (start us, length us, event | category | flops | bytes accessed | tf_op | source)
XLA Modules:
  0.0 124.5 jit_solution(12526739466642644304)
XLA Ops:
  0.0 0.0 copy-start
  0.0 121.7 %cadzow.1 = bf16[2,32,128,128]{3,2,1,0:T(8,128)(2,1)S(1)} custom-call(bf16[2,4096,128]{2,1,0:T(8,128)(2,1)} %bitcast.2, bf16[64,4096]{1,0:T(8,128)(2,1)} %bitcast.3), custom_call_target="tpu_custom_call" | custom-call | tf_op jit(solution)/shard_map/cadzow/pallas_call | solution.py:539
  121.7 0.0 copy-done
  121.7 2.9 %multiply_add_fusion = f32[2,32,128,128]{3,2,1,0:T(8,128)} fusion(bf16[2,32,128,128]{3,2,1,0:T(8,128)(2,1)S(1)} %cadzow.1, bf16[2,32,128,128]{3,2,1,0:T(8,128)(2,1)S(1)} %copy-done), kind=kLoop, calls=%fused_computation | loop fusion | flops 5242880 | bytes 8388608 | tf_op jit(solution)/shard_map/add | solution.py:550
Async XLA Ops:
  0.0 121.7 %copy-start = (bf16[2,32,128,128]{3,2,1,0:T(8,128)(2,1)S(1)}, bf16[2,32,128,128]{3,2,1,0:T(8,128)(2,1)}, u32[]{:S(2)}) copy-start(bf16[2,32,128,128]{3,2,1,0:T(8,128)(2,1)} %param.2) | copy-start | bytes 6291460
